TPU v7x, 32 devices: a whole 2x2x4 slice. The times are simulated.
32 devices in a mesh: outer: 8 (over z, core), inner: 4 (over y, x).
Axes of the slice: x: 2, y: 2, z: 4, core: 2. Of those that a mesh axis runs over, the one named last changes fastest.
Arguments:
- queries: bfloat16 [12288, 1536], P(('outer', 'inner')), may hold values from -6 to 6
- key_vectors: bfloat16 [12288, 1536], P(('outer', 'inner')), may hold values from -6 to 6
- value_vectors: bfloat16 [12288, 1536], P(('outer', 'inner')), may hold values from -6 to 6
- write_gate: float32 [12, 12288], P(None, ('outer', 'inner')), may hold values from 0.05 to 1
- ridge_term: float32 [12], replicated, may hold values from 0.25 to 4
- segment_ids: int32 [12288], P(('outer', 'inner')), may hold values from 0 to 15, never falling along the last dimension, each value on 1 to 1536 neighbouring positions
Outputs:
- mixed_heads: bfloat16 [12288, 1536], P(('outer', 'inner'))
Inputs may be any that keep to these rules, and one draw needn't show every extreme that they name: `segment_ids`: segment ids never fall along the tokens; each of the 16 documents spans 1 to 1536 tokens, one exactly 1536.
All inputs are finite; a program needn't handle non-finite values.
Results may differ from a plain program's by a relative error of at most 0.001.
Values sent between devices are 32-bit elements; how exact they have to be, the bound alone decides.
A program may use at most 64 MiB of HBM per device.

v0:
```python
import functools

import jax
import jax.numpy as jnp
from jax import lax
from jax.experimental import pallas as pl
from jax.experimental.pallas import tpu as pltpu
from jax.sharding import PartitionSpec as P

STRETCH = 128
ITERS = 4
PAIR = 2
MESH = pl.DeviceIdType.MESH
F32 = jnp.float32
BF16 = jnp.bfloat16


def split(x):
    hi = x.astype(BF16)
    return hi, (x - hi.astype(F32)).astype(BF16)


def mm(a, b):
    return jnp.dot(a, b, preferred_element_type=F32)


def same(a, b):
    return (a == b).astype(F32)


def kernel(
    sizes, q_far, k_far, v_far, gate_far, ridge_ref, seg_far, o_ref,
    q_ref, k_ref, v_ref, gate_ref, seg_ref, load_sem,
    causal, causal_t, keep, kt_buf, gram_row, memory_row, part,
    local, got1, pair, got2, suffix, got3, id_out, id_in,
    send1, recv1, send2, recv2, send3, recv3, id_send, id_recv,
):
    loads = [
        pltpu.make_async_copy(far, near, load_sem.at[i])
        for i, (far, near) in enumerate((
            (seg_far, seg_ref), (k_far, k_ref), (gate_far, gate_ref),
            (v_far, v_ref), (q_far, q_ref),
        ))
    ]
    for load in loads:
        load.start()
    outer, inner = sizes
    devices = outer * inner
    heads = gate_ref.shape[0]
    blocks = q_ref.shape[0] // STRETCH
    me = lax.axis_index("outer") * inner + lax.axis_index("inner")
    spot = me % 4
    odd_i, top_i = spot % 2, spot // 2

    def place(index):
        return (index // inner, index % inner)

    across1 = place(me + 1 - 2 * odd_i)
    across2 = place(me + 2 - 4 * top_i)
    after = place((me + 4) % devices)
    before = place((me + devices - 4) % devices)

    barrier = pltpu.get_barrier_semaphore()
    for target in (across1, across2, before):
        pl.semaphore_signal(barrier, inc=1, device_id=target, device_id_type=MESH)
    pl.semaphore_wait(barrier, 3)

    def exchange(src, dst, sender, receiver, target):
        return pltpu.make_async_remote_copy(
            src_ref=src, dst_ref=dst, send_sem=sender, recv_sem=receiver,
            device_id=target, device_id_type=MESH,
        )

    def phase1(h):
        return exchange(local.at[h], got1.at[h], send1.at[h], recv1.at[h], across1)

    def phase2(h):
        return exchange(pair.at[h], got2.at[h], send2.at[h], recv2.at[h], across2)

    def phase3(h):
        return exchange(suffix.at[h], got3.at[h], send3.at[h], recv3.at[h], after)

    def id_phase(p):
        target = (across1, across2, after)[p]
        return exchange(id_out.at[p], id_in.at[p], id_send.at[p], id_recv.at[p], target)

    loads[0].wait()
    seg = seg_ref[...].astype(F32)
    first = seg[0:1, 0:1]
    rows = [seg[b:b + 1, :] for b in range(blocks)]
    last = [seg[b:b + 1, STRETCH - 1:STRETCH] for b in range(blocks)]

    id_out[0] = jnp.broadcast_to(last[-1], (8, 128))
    id_phase(0).start()

    odd, top = odd_i.astype(F32), top_i.astype(F32)
    for b in range(blocks):
        grid_rows = jnp.broadcast_to(rows[b], (STRETCH, STRETCH))
        grid_cols = grid_rows.T
        down = lax.broadcasted_iota(jnp.int32, (STRETCH, STRETCH), 0)
        over = lax.broadcasted_iota(jnp.int32, (STRETCH, STRETCH), 1)
        causal[b] = jnp.where(over <= down, same(grid_rows, grid_cols), 0.0)
        causal_t[b] = causal[b].T
        keep[b] = same(grid_cols, first if b == 0 else last[b - 1]).astype(BF16)

    tails = [same(rows[b], last[b]) for b in range(blocks)]

    def columns(h):
        return pl.ds(pl.multiple_of(h * 128, 128), 128)

    def span(b):
        return slice(b * STRETCH, (b + 1) * STRETCH)

    def gather_local(h, carry):
        total = jnp.zeros((256, 128), F32)
        for b in range(blocks):
            keys = k_ref[span(b), columns(h)]
            values = v_ref[span(b), columns(h)]
            wide = keys.astype(F32).T
            kt_buf[h, b] = wide.astype(BF16)
            scale = lax.rsqrt(jnp.sum(wide * wide, axis=0, keepdims=True) + 1e-06)
            w1 = memory_row[h, b] * scale
            w2 = w1 * scale
            memory_row[h, b] = w1
            gram_row[h, b] = w2
            ghi, glo = split(wide * (w2 * tails[b]))
            mhi, mlo = split(wide * (w1 * tails[b]))
            gram = mm(jnp.concatenate([ghi, glo], 1), jnp.concatenate([keys, keys], 0))
            memory = mm(jnp.concatenate([mhi, mlo], 1), jnp.concatenate([values, values], 0))
            both = jnp.concatenate([gram, memory], 0)
            if b < blocks - 1:
                part[h, b] = both
            total = total + same(last[b], last[-1]) * both
        local[h] = total
        phase1(h).start()
        return carry

    for load in loads[1:4]:
        load.wait()
    for h in range(heads):
        for b in range(blocks):
            memory_row[h, b] = gate_ref[h:h + 1, span(b)]
    lax.fori_loop(0, 3, gather_local, 0)
    id_phase(0).wait_recv()
    other_last = id_in[0][0:1, 0:1]
    equal = same(last[-1], other_last)
    pair_local = odd + (1.0 - odd) * equal
    pair_got = (1.0 - odd) + odd * equal
    pair_id = odd * last[-1] + (1.0 - odd) * other_last
    id_out[1] = jnp.broadcast_to(pair_id, (8, 128))
    id_phase(1).start()
    lax.fori_loop(3, 5, gather_local, 0)
    id_phase(1).wait_recv()
    far_id = id_in[1][0:1, 0:1]
    base = top + (1.0 - top) * same(pair_id, far_id)
    suffix_local = base * (odd + (1.0 - odd) * pair_local)
    suffix_got = base * (1.0 - odd) * pair_got
    id_out[2] = jnp.broadcast_to(top * pair_id + (1.0 - top) * far_id, (8, 128))
    id_phase(2).start()

    def solve(base):
        items = [(base + i, b) for i in range(PAIR) for b in range(blocks)]
        every = range(len(items))
        mems, firsts, lows, seconds, weights, held, ridges = [], [], [], [], [], [], []
        xs, rs, ds, sqs = [], [], [], []
        state = None
        for h, b in items:
            if b == 0:
                state = in1 * got1[h] + in2 * got2[h] + in3 * got3[h]
            else:
                previous = first if b == 1 else last[b - 2]
                state = part[h, b - 1] + same(last[b - 1], previous) * state
            hi, lo = split(state)
            k = k_ref[span(b), columns(h)]
            v = v_ref[span(b), columns(h)]
            kt = kt_buf[h, b]
            firsts.append(jnp.concatenate([k, hi[:128]], 0))
            lows.append(lo[:128])
            seconds.append(jnp.concatenate([kt, kt], 1))
            mems.append(jnp.concatenate([v, v, hi[128:], hi[128:], lo[128:]], 0))
            column = jnp.broadcast_to(gram_row[h, b], (8, STRETCH)).T[:, 0:1]
            weights.append(causal_t[b] * column)
            held.append(same(rows[b], first if b == 0 else last[b - 1]))
            ridges.append(ridge_ref[h])
            q = q_ref[span(b), columns(h)].astype(F32).T
            q = q * lax.rsqrt(jnp.sum(q * q, axis=0, keepdims=True) + 1e-06)
            rs.append(q)
            ds.append(q)
            sqs.append(jnp.sum(q * q, axis=0, keepdims=True))

        for sweep in range(ITERS - 1):
            cuts = [split(ds[c]) for c in every]
            raised = [
                mm(jnp.concatenate([firsts[c]] * 2, 1), jnp.concatenate(cuts[c], 0)) for c in every
            ]
            lowered = [mm(lows[c], cuts[c][0]) for c in every]
            scores = [split(raised[c][:128] * weights[c]) for c in every]
            inside = [mm(seconds[c], jnp.concatenate(scores[c], 0)) for c in every]
            for c in every:
                d = ds[c]
                image = inside[c] + held[c] * (raised[c][128:] + lowered[c]) + ridges[c] * d
                size = sqs[c] / jnp.sum(d * image, axis=0, keepdims=True)
                if sweep == 0:
                    xs.append(size * d)
                else:
                    xs[c] = xs[c] + size * d
                rs[c] = rs[c] - size * image
                fresh = jnp.sum(rs[c] * rs[c], axis=0, keepdims=True)
                ds[c] = rs[c] + fresh / sqs[c] * d
                sqs[c] = fresh
        raised = [mm(firsts[c], ds[c].astype(BF16)) for c in every]
        for c in every:
            d, scores = ds[c], raised[c][:128]
            form = scores * scores * weights[c] + d * (held[c] * raised[c][128:] + ridges[c] * d)
            xs[c] = xs[c] + sqs[c] / jnp.sum(form, axis=0, keepdims=True) * d

        cuts = [split(xs[c].T) for c in every]
        scores = []
        for c, (h, b) in enumerate(items):
            kt = kt_buf[h, b]
            scores.append(mm(jnp.concatenate(cuts[c], 1), jnp.concatenate([kt, kt], 0)))
        for c, (h, b) in enumerate(items):
            shi, slo = split(scores[c] * (causal[b] * memory_row[h, b]))
            hi, lo = cuts[c]
            mask = keep[b]
            khi, klo = hi * mask, lo * mask
            out = mm(jnp.concatenate([shi, slo, khi, klo, khi], 1), mems[c])
            o_ref[span(b), columns(h)] = out.astype(BF16)

    def relay1(h):
        phase1(h).wait_recv()
        pair[h] = pair_local * local[h] + pair_got * got1[h]
        phase2(h).start()

    def relay2(h):
        phase2(h).wait_recv()
        suffix[h] = (1.0 - top) * got2[h] + suffix_local * local[h] + suffix_got * got1[h]
        phase3(h).start()

    relay1(0)
    lax.fori_loop(5, 8, gather_local, 0)
    relay1(1)
    lax.fori_loop(8, heads, gather_local, 0)
    relay1(2)
    loads[4].wait()
    id_phase(2).wait_recv()
    in1 = odd * same(other_last, first)
    in2 = top * same(far_id, first)
    in3 = same(id_in[2][0:1, 0:1], first)
    relay1(3)
    relay2(0)
    relay2(1)
    groups = heads // PAIR

    def stage(t, carry):
        @pl.when(t < groups - 2)
        def _():
            for i in range(PAIR):
                relay1(PAIR * (t + 2) + i)

        @pl.when(t < groups - 1)
        def _():
            for i in range(PAIR):
                relay2(PAIR * (t + 1) + i)

        for i in range(PAIR):
            phase3(PAIR * t + i).wait_recv()
        solve(PAIR * t)
        return carry

    lax.fori_loop(0, groups, stage, 0)

    def drain(h, carry):
        phase1(h).wait_send()
        phase2(h).wait_send()
        phase3(h).wait_send()
        return carry

    lax.fori_loop(0, heads, drain, 0)
    for p in range(3):
        id_phase(p).wait_send()


def body(sizes, queries, key_vectors, value_vectors, write_gate, ridge_term, segment_ids):
    tokens, width = queries.shape
    heads = ridge_term.shape[0]
    blocks = tokens // STRETCH
    vmem = pl.BlockSpec(memory_space=pltpu.VMEM)
    far = pl.BlockSpec(memory_space=pl.ANY)
    smem = pl.BlockSpec(memory_space=pltpu.SMEM)
    state = pltpu.VMEM((heads, 256, 128), F32)
    return pl.pallas_call(
        functools.partial(kernel, sizes),
        out_shape=jax.ShapeDtypeStruct((tokens, width), BF16),
        in_specs=[far, far, far, far, smem, far],
        out_specs=vmem,
        scratch_shapes=[
            pltpu.VMEM((tokens, width), BF16),
            pltpu.VMEM((tokens, width), BF16),
            pltpu.VMEM((tokens, width), BF16),
            pltpu.VMEM((heads, tokens), F32),
            pltpu.VMEM((blocks, STRETCH), jnp.int32),
            pltpu.SemaphoreType.DMA((5,)),
            pltpu.VMEM((blocks, STRETCH, STRETCH), F32),
            pltpu.VMEM((blocks, STRETCH, STRETCH), F32),
            pltpu.VMEM((blocks, STRETCH, STRETCH), BF16),
            pltpu.VMEM((heads, blocks, 128, STRETCH), BF16),
            pltpu.VMEM((heads, blocks, 1, STRETCH), F32),
            pltpu.VMEM((heads, blocks, 1, STRETCH), F32),
            pltpu.VMEM((heads, blocks - 1, 256, 128), F32),
            state, state, state, state, state, state,
            pltpu.VMEM((3, 8, 128), F32),
            pltpu.VMEM((3, 8, 128), F32),
        ] + [pltpu.SemaphoreType.DMA((heads,))] * 6 + [pltpu.SemaphoreType.DMA((3,))] * 2,
        compiler_params=pltpu.CompilerParams(
            collective_id=0, has_side_effects=True, vmem_limit_bytes=60 * 1024 * 1024
        ),
        cost_estimate=pl.CostEstimate(
            flops=6_000_000_000, bytes_accessed=6_000_000, transcendentals=0
        ),
    )(
        queries, key_vectors, value_vectors, write_gate, ridge_term,
        segment_ids.reshape(blocks, STRETCH),
    )


def solution(mesh):
    sizes = (mesh.shape["outer"], mesh.shape["inner"])
    return jax.shard_map(
        functools.partial(body, sizes),
        mesh=mesh,
        in_specs=(
            P(("outer", "inner"), None),
            P(("outer", "inner"), None),
            P(("outer", "inner"), None),
            P(None, ("outer", "inner")),
            P(),
            P(("outer", "inner")),
        ),
        out_specs=P(("outer", "inner"), None),
        check_vma=False,
    )
```

profile of v0, /device:TPU:0, one launch (start us, length us, event | category | flops | bytes accessed | tf_op | source)
XLA Modules:
  0.0 57.3 jit_solution(8324807306051022173)
XLA Ops:
  0.0 55.0 %shard_map.64 = bf16[384,1536]{1,0:T(8,128)(2,1)} custom-call(bf16[384,1536]{1,0:T(8,128)(2,1)} %q_far.1, bf16[384,1536]{1,0:T(8,128)(2,1)} %k_far.1, bf16[384,1536]{1,0:T(8,128)(2,1)} %v_far.1, f32[12,384]{1,0:T(8,128)} %gate_far.1, f32[12]{0:T(128)} %ridge_ref.1, s32[3,128]{1,0:T(4,128)} %bitcast.1), custom_call_target="tpu_custom_call" | custom-call | flops 6000000000 | bytes 6000000 | tf_op jit(solution)/shard_map/pallas_call | solution.py:292
  55.0 2.4 %copy.8 = bf16[384,1536]{1,0:T(8,128)(2,1)} copy(bf16[384,1536]{1,0:T(8,128)(2,1)} %shard_map.64) | data formatting | bytes 2359296
where the time goes:
time: 57.5 us; the launch traced here: 57.3 us
  Pallas kernels  55 us (96%)
  local copies, waits for them, and re-layouts  2.36 us (4%)
    pallas_call x1, Pallas kernels, body(): pl.pallas_call(functools.partial(kernel, sizes), out_shape=jax.ShapeDtype...  55 us
    unnamed x1, local copies, waits for them, and re-layouts  2.36 us

commit v1 on v0

--- a/solution.py
+++ b/solution.py
@@ -111,6 +111,18 @@
     def span(b):
         return slice(b * STRETCH, (b + 1) * STRETCH)
 
+    half_down = lax.broadcasted_iota(jnp.int32, (64, 128), 0)
+    half_over = lax.broadcasted_iota(jnp.int32, (64, 128), 1)
+
+    def square(packed):
+        flat = packed[128:192]
+        turned = jnp.concatenate([flat, jnp.zeros_like(flat)], 0).T
+        upper = jnp.where(half_down <= half_over, flat, turned[0:64])
+        low = jnp.where(half_down > half_over, flat, turned[0:64])
+        low = jnp.where(half_down == half_over, packed[192:193], low)
+        lower = jnp.where(half_over < 64, turned[64:128], pltpu.roll(low, 64, 1))
+        return jnp.concatenate([upper, lower, packed[0:128]], 0)
+
     def gather_local(h, carry):
         total = jnp.zeros((256, 128), F32)
         for b in range(blocks):
@@ -131,7 +143,11 @@
             if b < blocks - 1:
                 part[h, b] = both
             total = total + same(last[b], last[-1]) * both
-        local[h] = total
+        low = pltpu.roll(total[64:128], 64, 1)
+        local[h, 0:128] = total[128:256]
+        local[h, 128:192] = jnp.where(half_down > half_over, low, total[0:64])
+        corner = jnp.sum(jnp.where(half_down == half_over, low, 0.0), axis=0, keepdims=True)
+        local[h, 192:200] = jnp.broadcast_to(corner, (8, 128))
         phase1(h).start()
         return carry
 
@@ -166,7 +182,7 @@
         state = None
         for h, b in items:
             if b == 0:
-                state = in1 * got1[h] + in2 * got2[h] + in3 * got3[h]
+                state = square(in1 * got1[h] + in2 * got2[h] + in3 * got3[h])
             else:
                 previous = first if b == 1 else last[b - 2]
                 state = part[h, b - 1] + same(last[b - 1], previous) * state
@@ -288,7 +304,7 @@
     vmem = pl.BlockSpec(memory_space=pltpu.VMEM)
     far = pl.BlockSpec(memory_space=pl.ANY)
     smem = pl.BlockSpec(memory_space=pltpu.SMEM)
-    state = pltpu.VMEM((heads, 256, 128), F32)
+    state = pltpu.VMEM((heads, 200, 128), F32)
     return pl.pallas_call(
         functools.partial(kernel, sizes),
         out_shape=jax.ShapeDtypeStruct((tokens, width), BF16),

time: 57.5 us -> 48.9 us (0.85)
  Pallas kernels: 55 us -> 46.4 us
    pallas_call x1, Pallas kernels: 55 us -> 46.4 us  [body(): pl.pallas_call(functools.partial(kernel, sizes), out_shape=jax.ShapeDtype...]
where the time goes in v1:
time: 48.9 us; the launch traced here: 48.8 us
  Pallas kernels  46.4 us (95%)
  local copies, waits for them, and re-layouts  2.36 us (5%)
    pallas_call x1, Pallas kernels, body(): pl.pallas_call(functools.partial(kernel, sizes), out_shape=jax.ShapeDtype...  46.4 us
    unnamed x1, local copies, waits for them, and re-layouts  2.36 us

profile of v1, /device:TPU:0, one launch (start us, length us, event | category | flops | bytes accessed | tf_op | source)
XLA Modules:
  0.0 48.8 jit_solution(16749533336843509315)
XLA Ops:
  0.0 46.4 %shard_map.64 = bf16[384,1536]{1,0:T(8,128)(2,1)} custom-call(bf16[384,1536]{1,0:T(8,128)(2,1)} %q_far.1, bf16[384,1536]{1,0:T(8,128)(2,1)} %k_far.1, bf16[384,1536]{1,0:T(8,128)(2,1)} %v_far.1, f32[12,384]{1,0:T(8,128)} %gate_far.1, f32[12]{0:T(128)} %ridge_ref.1, s32[3,128]{1,0:T(4,128)} %bitcast.1), custom_call_target="tpu_custom_call" | custom-call | flops 6000000000 | bytes 6000000 | tf_op jit(solution)/shard_map/pallas_call | solution.py:308
  46.4 2.4 %copy.8 = bf16[384,1536]{1,0:T(8,128)(2,1)} copy(bf16[384,1536]{1,0:T(8,128)(2,1)} %shard_map.64) | data formatting | bytes 2359296

commit v2 on v1

--- a/solution.py
+++ b/solution.py
@@ -174,8 +174,8 @@
     id_out[2] = jnp.broadcast_to(top * pair_id + (1.0 - top) * far_id, (8, 128))
     id_phase(2).start()
 
-    def solve(base):
-        items = [(base + i, b) for i in range(PAIR) for b in range(blocks)]
+    def solve(t):
+        items = [(PAIR * t + i, b) for i in range(PAIR) for b in range(blocks)]
         every = range(len(items))
         mems, firsts, lows, seconds, weights, held, ridges = [], [], [], [], [], [], []
         xs, rs, ds, sqs = [], [], [], []
@@ -224,6 +224,16 @@
                 fresh = jnp.sum(rs[c] * rs[c], axis=0, keepdims=True)
                 ds[c] = rs[c] + fresh / sqs[c] * d
                 sqs[c] = fresh
+            if sweep == 0:
+                @pl.when(t < groups - 2)
+                def _():
+                    for i in range(PAIR):
+                        relay1(PAIR * (t + 2) + i)
+            if sweep == 1:
+                @pl.when(t < groups - 1)
+                def _():
+                    for i in range(PAIR):
+                        relay2(PAIR * (t + 1) + i)
         raised = [mm(firsts[c], ds[c].astype(BF16)) for c in every]
         for c in every:
             d, scores = ds[c], raised[c][:128]
@@ -263,25 +273,15 @@
     in1 = odd * same(other_last, first)
     in2 = top * same(far_id, first)
     in3 = same(id_in[2][0:1, 0:1], first)
-    relay1(3)
     relay2(0)
     relay2(1)
+    relay1(3)
     groups = heads // PAIR
 
     def stage(t, carry):
-        @pl.when(t < groups - 2)
-        def _():
-            for i in range(PAIR):
-                relay1(PAIR * (t + 2) + i)
-
-        @pl.when(t < groups - 1)
-        def _():
-            for i in range(PAIR):
-                relay2(PAIR * (t + 1) + i)
-
         for i in range(PAIR):
             phase3(PAIR * t + i).wait_recv()
-        solve(PAIR * t)
+        solve(t)
         return carry
 
     lax.fori_loop(0, groups, stage, 0)

time: 48.9 us -> 52.4 us (1.072)
  Pallas kernels: 46.4 us -> 49.8 us
    pallas_call x1, Pallas kernels: 46.4 us -> 49.8 us  [body(): pl.pallas_call(functools.partial(kernel, sizes), out_shape=jax.ShapeDtype...]
where the time goes in v2:
time: 52.4 us; the launch traced here: 52.2 us
  Pallas kernels  49.8 us (95%)
  local copies, waits for them, and re-layouts  2.36 us (5%)
    pallas_call x1, Pallas kernels, body(): pl.pallas_call(functools.partial(kernel, sizes), out_shape=jax.ShapeDtype...  49.8 us
    unnamed x1, local copies, waits for them, and re-layouts  2.36 us

profile of v2, /device:TPU:0, one launch (start us, length us, event | category | flops | bytes accessed | tf_op | source)
XLA Modules:
  0.0 52.2 jit_solution(9445488219945484903)
XLA Ops:
  0.0 49.8 %shard_map.64 = bf16[384,1536]{1,0:T(8,128)(2,1)} custom-call(bf16[384,1536]{1,0:T(8,128)(2,1)} %q_far.1, bf16[384,1536]{1,0:T(8,128)(2,1)} %k_far.1, bf16[384,1536]{1,0:T(8,128)(2,1)} %v_far.1, f32[12,384]{1,0:T(8,128)} %gate_far.1, f32[12]{0:T(128)} %ridge_ref.1, s32[3,128]{1,0:T(4,128)} %bitcast.1), custom_call_target="tpu_custom_call" | custom-call | flops 6000000000 | bytes 6000000 | tf_op jit(solution)/shard_map/pallas_call | solution.py:308
  49.8 2.4 %copy.8 = bf16[384,1536]{1,0:T(8,128)(2,1)} copy(bf16[384,1536]{1,0:T(8,128)(2,1)} %shard_map.64) | data formatting | bytes 2359296

commit v3 on v1

--- a/solution.py
+++ b/solution.py
@@ -263,21 +263,21 @@
     in1 = odd * same(other_last, first)
     in2 = top * same(far_id, first)
     in3 = same(id_in[2][0:1, 0:1], first)
-    relay1(3)
     relay2(0)
     relay2(1)
+    relay1(3)
     groups = heads // PAIR
 
     def stage(t, carry):
+        @pl.when(t < groups - 1)
+        def _():
+            for i in range(PAIR):
+                relay2(PAIR * (t + 1) + i)
+
         @pl.when(t < groups - 2)
         def _():
             for i in range(PAIR):
                 relay1(PAIR * (t + 2) + i)
-
-        @pl.when(t < groups - 1)
-        def _():
-            for i in range(PAIR):
-                relay2(PAIR * (t + 1) + i)
 
         for i in range(PAIR):
             phase3(PAIR * t + i).wait_recv()

time: 48.9 us -> 51.6 us (1.055)
  the two profiles are of different devices: /device:TPU:0 before, /device:TPU:24 now
where the time goes in v3:
time: 51.6 us; the launch traced here: 51.4 us
  Pallas kernels  49.1 us (95%)
  local copies, waits for them, and re-layouts  2.36 us (5%)
    pallas_call x1, Pallas kernels, body(): pl.pallas_call(functools.partial(kernel, sizes), out_shape=jax.ShapeDtype...  49.1 us
    unnamed x1, local copies, waits for them, and re-layouts  2.36 us

profile of v3, /device:TPU:24, one launch (start us, length us, event | category | flops | bytes accessed | tf_op | source)
XLA Modules:
  0.0 51.4 jit_solution(8646248486421077237)
XLA Ops:
  0.0 49.1 %shard_map.64 = bf16[384,1536]{1,0:T(8,128)(2,1)} custom-call(bf16[384,1536]{1,0:T(8,128)(2,1)} %q_far.1, bf16[384,1536]{1,0:T(8,128)(2,1)} %k_far.1, bf16[384,1536]{1,0:T(8,128)(2,1)} %v_far.1, f32[12,384]{1,0:T(8,128)} %gate_far.1, f32[12]{0:T(128)} %ridge_ref.1, s32[3,128]{1,0:T(4,128)} %bitcast.1), custom_call_target="tpu_custom_call" | custom-call | flops 6000000000 | bytes 6000000 | tf_op jit(solution)/shard_map/pallas_call | solution.py:308
  49.1 2.4 %copy.8 = bf16[384,1536]{1,0:T(8,128)(2,1)} copy(bf16[384,1536]{1,0:T(8,128)(2,1)} %shard_map.64) | data formatting | bytes 2359296
